TPU v7x, 32 devices: a whole 2x2x4 slice. The times are simulated.
32 devices in a mesh: band: 2 (over x), stn: 8 (over z, y), tm: 2 (over core).
Axes of the slice: x: 2, y: 2, z: 4, core: 2. Of those that a mesh axis runs over, the one named last changes fastest.
Arguments:
- voltages: int32 [704, 4, 32768], P('stn', 'band', 'tm'), parts along dimension 1, may hold values from -125 to 125, as said below
- filter_taps: float32 [16, 128], replicated, may hold values from -0.036 to 0.036
Outputs:
- visibilities: float32 [2, 2, 128, 704, 704], P(None, None, ('band', 'stn', 'tm')), parts along dimension 2
There are 2 independent parts, one for each index of `band`. A program takes and returns all parts, laid end to end along the dimension named above; an argument that names none is the same for every part. Nothing has to cross between parts.
Inputs may be any that keep to these rules, and one draw needn't show every extreme that they name: `voltages`: each input's samples are an integer gain of -2 to 2 times a signal common to all inputs plus noise of its own.
All inputs are finite; a program needn't handle non-finite values.
Results may differ from a plain program's by a relative error of at most 0.00049.
Values may be sent and summed in bfloat16 or wider, within the bound.
A program may use at most 192 MiB of HBM per device.

v0:
```python
import math
import jax
import jax.numpy as jnp
from jax import lax
from jax.sharding import PartitionSpec as P


def passed_along(value, axis, steps):
    count = lax.axis_size(axis)
    pairs = [(source, (source + steps) % count) for source in range(count)]
    return lax.ppermute(value, axis, pairs)


def transform_table(frame_len, chan_count):
    sample_index = jnp.arange(frame_len, dtype=jnp.int32)[:, None]
    chan_index = jnp.arange(chan_count, dtype=jnp.int32)[None, :]
    phase = (2 * chan_index + 1) * sample_index % (2 * frame_len)
    angle = phase.astype(jnp.float32) * (math.pi / frame_len)
    factor = 1.0 / math.sqrt(frame_len)
    cosine = jnp.cos(angle) * factor
    sine = -jnp.sin(angle) * factor
    return jnp.stack([cosine, sine], axis=2).reshape(frame_len, 2 * chan_count)


def arrange(blocks):
    stations, blocks_time, per_dev, parts_two, inputs_dev, sub_count, spec_dev = blocks.shape
    ordered = jnp.transpose(blocks, (3, 5, 2, 0, 4, 1, 6))
    return ordered.reshape(
        parts_two, sub_count, per_dev, stations * inputs_dev, blocks_time * spec_dev
    )


def correlate(stacked):
    real_in = stacked[0]
    imag_in = stacked[1]
    right_side = jnp.concatenate([real_in, imag_in], axis=-1)
    left_imag = jnp.concatenate([imag_in, -real_in], axis=-1)
    real_part = jnp.einsum(
        "gcis,gcjs->gcij", right_side, right_side, preferred_element_type=jnp.float32
    )
    imag_part = jnp.einsum(
        "gcis,gcjs->gcij", left_imag, right_side, preferred_element_type=jnp.float32
    )
    return jnp.stack([real_part, imag_part])


def shards(voltages, filter_taps):
    inputs_dev, sub_count, time_dev = voltages.shape
    taps_count, frame_len = filter_taps.shape
    spec_dev = time_dev // frame_len
    chan_count = frame_len // 2
    lagging = taps_count - 1
    frames = voltages.astype(jnp.bfloat16).reshape(inputs_dev, sub_count, spec_dev, frame_len)
    last_frames = frames[:, :, spec_dev - lagging :, :]
    received = passed_along(last_frames, "tm", 1)
    earlier = jnp.concatenate([jnp.zeros_like(received[:, :1]), received[:, :-1]], axis=1)
    history = jnp.where(lax.axis_index("tm") == 0, earlier, received)
    extended = jnp.concatenate([history, frames], axis=2).astype(jnp.float32)
    filtered = filter_taps[0] * extended[:, :, 0:spec_dev]
    for tap_index in range(1, taps_count):
        filtered = (
            filtered + filter_taps[tap_index] * extended[:, :, tap_index : tap_index + spec_dev]
        )
    table = transform_table(frame_len, chan_count)
    spectra = lax.dot_general(
        table,
        filtered.reshape(-1, frame_len),
        (((0,), (1,)), ((), ())),
        precision=lax.Precision.HIGHEST,
        preferred_element_type=jnp.float32,
    ).astype(jnp.bfloat16)
    stations = lax.axis_size("stn")
    halves = lax.axis_size("tm")
    scale = 1.0 / (spec_dev * halves)
    moved = lax.all_to_all(spectra[None], ("stn", "tm"), split_axis=1, concat_axis=0, tiled=True)
    per_dev = moved.shape[1] // 2
    blocks = moved.reshape(stations, halves, per_dev, 2, inputs_dev, sub_count, spec_dev)
    result = correlate(arrange(blocks))
    return result * scale


def solution(mesh):
    placed = (P("stn", "band", "tm"), P())
    return jax.shard_map(
        shards,
        mesh=mesh,
        in_specs=placed,
        out_specs=P(None, None, ("band", "stn", "tm"), None, None),
        check_vma=False,
    )
```

profile of v0, /device:TPU:1, one launch (start us, length us, event | category | flops | bytes accessed | tf_op | source)
XLA Modules:
  0.0 507.7 jit_solution(10586503539075918280)
XLA Ops:
  0.0 9.0 %convert_element_type.26 = bf16[88,2,16384]{2,1,0:T(2,128)(2,1)} convert(s32[88,2,16384]{2,1,0:T(2,128)} %param.2) | non-fusion elementwise | flops 2883584 | bytes 17301504 | tf_op jit(solution)/shard_map/convert_element_type | solution.py:53
  9.0 10.5 %reshape.154 = bf16[88,2,128,128]{3,2,1,0:T(8,128)(2,1)} reshape(bf16[88,2,16384]{2,1,0:T(2,128)(2,1)} %convert_element_type.26) | data formatting | bytes 11534336 | tf_op jit(solution)/shard_map/reshape | solution.py:53
  19.5 1.4 slice.146
  20.9 0.1 copy.33
  21.1 0.2 copy.19
  21.3 0.1 collective-permute-start
  21.4 0.2 cosine_multiply_fusion
  21.7 1.7 collective-permute-done
  23.5 0.1 copy.28
  23.6 0.2 pad_select_fusion
  23.7 10.6 %maximum_convert_fusion = f32[88,2,143,128]{3,2,0,1:T(8,128)} fusion(bf16[88,2,15,128]{3,2,0,1:T(8,128)(2,1)S(1)} %pad_select_fusion, bf16[88,2,128,128]{3,2,1,0:T(8,128)(2,1)} %reshape.154), kind=kLoop, calls=%fused_computation.36 | loop fusion | flops 12886016 | bytes 19329024 | tf_op jit(solution)/shard_map/convert_element_type | solution.py:58
  34.3 74.6 %fusion.1 = f32[88,2,128,128]{3,2,0,1:T(8,128)} fusion(f32[88,2,143,128]{3,2,0,1:T(8,128)} %maximum_convert_fusion, f32[128]{0:T(128)S(1)} %get-tuple-element.23, f32[128]{0:T(128)S(1)} %get-tuple-element.24, f32[128]{0:T(128)S(1)} %get-tuple-element.10, f32[128]{0:T(128)S(1)} %get-tuple-element.11, f32[128]{0:T(128)S(1)} %get-tuple-element.12, ...), kind=kLoop, calls=%fused_computation.4 | loop fusion | flops 89391104 | bytes 196091904 | tf_op jit(solution)/shard_map/add | solution.py:62
  109.0 10.6 %copy.22 = f32[88,2,128,128]{3,2,1,0:T(8,128)} copy(f32[88,2,128,128]{3,2,0,1:T(8,128)} %fusion.1) | data formatting | bytes 23068672 | tf_op jit(solution)/shard_map/add | solution.py:62
  119.6 13.6 %fusion = bf16[1,128,22528]{2,1,0:T(8,128)(2,1)S(1)} fusion(f32[128,128]{0,1:T(8,128)S(1)} %bitcast.54, f32[22528,128]{1,0:T(8,128)} %bitcast.52), kind=kOutput, calls=%fused_computation.2 | convolution fusion | flops 4432068608 | bytes 17367040 | tf_op jit(solution)/shard_map/dot_general | solution.py:65
  133.2 47.5 %copy.32 = bf16[1,128,22528]{2,0,1:T(2,128)(2,1)} copy(bf16[1,128,22528]{2,1,0:T(8,128)(2,1)S(1)} %fusion) | data formatting | bytes 11534336 | tf_op jit(solution)/shard_map/broadcast_in_dim | solution.py:75
  180.7 0.6 broadcast.142
  181.3 35.9 %reduce.2 = bf16[128,22528]{1,0:T(8,128)(2,1)} reduce(bf16[128,1,22528]{2,1,0:T(2,128)(2,1)} %bitcast.51, bf16[]{:T(256)} %broadcast.142), dimensions={1}, to_apply=%bitcast.50.reduce_sub_computation | reduce | bytes 11534338
  217.2 13.4 %reshape.156 = bf16[16,2,90112]{2,1,0:T(2,128)(2,1)} reshape(bf16[128,22528]{1,0:T(8,128)(2,1)} %reduce.2) | data formatting | bytes 11534336
  230.5 133.9 %all_to_all.4 = bf16[16,2,90112]{2,1,0:T(2,128)(2,1)} all-to-all(bf16[16,2,90112]{2,1,0:T(2,128)(2,1)} %reshape.156), channel_id=1, replica_groups=mesh['band'=2,'stn'=8,'tm'=2] {'stn','tm'}, dimensions={0} | all-to-all | bytes 11534336 | tf_op jit(solution)/shard_map/all_to_all | solution.py:75
  364.5 13.8 %reshape.157 = bf16[128,1,22528]{2,1,0:T(2,128)(2,1)} reshape(bf16[16,2,90112]{2,1,0:T(2,128)(2,1)} %all_to_all.4) | data formatting | bytes 11534336
  378.3 36.0 %bitcast_reduce_fusion = bf16[128,22528]{1,0:T(8,128)(2,1)} fusion(bf16[128,1,22528]{2,1,0:T(2,128)(2,1)} %reshape.157), kind=kLoop, calls=%fused_computation.75 | loop fusion | bytes 11534336 | tf_op jit(solution)/shard_map/all_to_all | solution.py:75
  414.3 8.9 %reshape.153 = bf16[8,2,4,2,88,2,128]{6,5,4,3,2,1,0:T(2,128)(2,1)} reshape(bf16[128,22528]{1,0:T(8,128)(2,1)} %bitcast_reduce_fusion) | data formatting | bytes 11534336 | tf_op jit(solution)/shard_map/reshape | solution.py:77
  423.2 8.4 %fusion.26 = (bf16[1,2,4,8,88,2,128]{6,1,4,0,2,5,3:T(2,128)(2,1)S(1)}, bf16[1,2,4,8,88,2,128]{6,1,4,0,2,5,3:T(2,128)(2,1)}) fusion(bf16[2,2,4,8,88,2,128]{6,1,4,0,2,5,3:T(2,128)(2,1)} %bitcast.53), kind=kLoop, calls=%fused_computation.73 | loop fusion | bytes 11534336 | tf_op jit(solution)/shard_map/slice | solution.py:35
  431.7 4.5 copy.25
  436.2 6.5 %squeeze.7 = bf16[2,4,704,256]{3,2,1,0:T(8,128)(2,1)S(1)} reshape(bf16[1,2,4,8,88,2,128]{6,5,4,3,2,1,0:T(2,128)(2,1)} %copy.25) | data formatting | bytes 5767168 | tf_op jit(solution)/shard_map/squeeze | solution.py:35
  442.8 6.4 %copy.24 = bf16[1,2,4,8,88,2,128]{6,5,4,3,2,1,0:T(2,128)(2,1)} copy(bf16[1,2,4,8,88,2,128]{6,1,4,0,2,5,3:T(2,128)(2,1)} %get-tuple-element.6) | data formatting | bytes 5767168 | tf_op jit(solution)/shard_map/slice | solution.py:34
  449.1 7.4 %squeeze.6 = bf16[2,4,704,256]{3,2,1,0:T(8,128)(2,1)} reshape(bf16[1,2,4,8,88,2,128]{6,5,4,3,2,1,0:T(2,128)(2,1)} %copy.24) | data formatting | bytes 5767168 | tf_op jit(solution)/shard_map/squeeze | solution.py:34
  456.6 5.0 fusion.27
  461.6 0.2 constant_dynamic-update-slice_fusion
  461.9 8.4 %convolution_bitcast_fusion.1 = f32[1,2,4,704,704]{4,3,2,1,0:T(8,128)} fusion(bf16[2,4,704,512]{3,2,1,0:T(8,128)(2,1)S(1)} %constant_dynamic-update-slice_fusion), kind=kOutput, calls=%fused_computation.35 | convolution fusion | flops 4060086272 | bytes 21626880 | tf_op jit(solution)/shard_map/gcis,gcjs->gcij/dot_general | solution.py:38
  470.3 14.1 %convolution_bitcast_fusion = f32[1,2,4,704,704]{4,3,2,1,0:T(8,128)} fusion(bf16[2,4,704,512]{3,2,1,0:T(8,128)(2,1)} %copy-done, bf16[2,4,704,256]{3,2,1,0:T(8,128)(2,1)} %get-tuple-element.7, bf16[2,4,704,256]{3,2,1,0:T(8,128)(2,1)S(1)} %squeeze.7), kind=kOutput, calls=%fused_computation.34 | convolution fusion | flops 4071620608 | bytes 27394048 | tf_op jit(solution)/shard_map/gcis,gcjs->gcij/dot_general | solution.py:41
  484.4 23.2 %maximum_multiply_fusion = f32[2,2,4,704,704]{4,3,2,1,0:T(8,128)} fusion(f32[1,2,4,704,704]{4,3,2,1,0:T(8,128)} %convolution_bitcast_fusion, f32[1,2,4,704,704]{4,3,2,1,0:T(8,128)} %convolution_bitcast_fusion.1), kind=kLoop, calls=%fused_computation | loop fusion | flops 15859712 | bytes 63438848 | tf_op jit(solution)/shard_map/mul | solution.py:79
  (9 shorter events, 0.1 us)
Async XLA Ops:
  9.0 12.7 %copy-start.1 = (f32[16,128]{1,0:T(8,128)S(1)}, f32[16,128]{1,0:T(8,128)}, u32[]{:S(2)}) copy-start(f32[16,128]{1,0:T(8,128)} %param.3) | copy-start | bytes 24580
  21.3 2.2 collective-permute-start
  461.8 8.4 %copy-start = (bf16[2,4,704,512]{3,2,1,0:T(8,128)(2,1)}, bf16[2,4,704,512]{3,2,1,0:T(8,128)(2,1)S(1)}, u32[]{:S(2)}) copy-start(bf16[2,4,704,512]{3,2,1,0:T(8,128)(2,1)S(1)} %constant_dynamic-update-slice_fusion) | copy-start | bytes 17301508
where the time goes:
time: 516 us; the launch traced here: 508 us
  local copies, waits for them, and re-layouts  177 us (34%)
  other arithmetic  159 us (31%)
  blocking collectives  134 us (26%)
  matrix products  36.1 us (7%)
    all_to_all x1, blocking collectives, shards(): lax.all_to_all(spectra[None], ('stn', 'tm'), split_axis=1, concat_axis=0,...  134 us
    add x1, other arithmetic, shards(): filtered + filter_taps[tap_index] * extended[:, :, tap_index:tap_index +...  74.6 us
    broadcast_in_dim x1, local copies, waits for them, and re-layouts, shards(): spectra[None]  47.5 us
    all_to_all x1, local copies, waits for them, and re-layouts, shards(): lax.all_to_all(spectra[None], ('stn', 'tm'), split_axis=1, concat_axis=0,...  36 us
    unnamed x1, other arithmetic  35.9 us
    unnamed x9, local copies, waits for them, and re-layouts  28 us
    mul x1, other arithmetic, shards(): return result * scale  23.2 us
    dot_general x1, matrix products, correlate(): jnp.einsum('gcis,gcjs->gcij', left_imag, right_side, preferred_element_ty...  14.1 us
  transfers between devices with their start and end apart: 1, of which 1 were waited for; matrix products, arithmetic and copies ran while one was open for 0% of the time, Pallas kernels for 0%

commit v1 on v0

--- a/solution.py
+++ b/solution.py
@@ -3,6 +3,23 @@
 import jax.numpy as jnp
 from jax import lax
 from jax.sharding import PartitionSpec as P
+from jax.lax import axis_index, axis_size, ppermute
+
+
+def load_frames(xs, on_dim, my_data):
+    part_next = xs.shape
+    latest = xs.reshape(
+        *part_next[:on_dim], my_data, part_next[on_dim] // my_data, *part_next[on_dim + 1 :]
+    )
+    return jnp.moveaxis(latest, on_dim, 0)
+
+
+def detail_quotas_over_axis(work_x, join_dim):
+    work_x = jnp.moveaxis(work_x, 0, join_dim)
+    lower = work_x.shape
+    return work_x.reshape(
+        *lower[:join_dim], lower[join_dim] * lower[join_dim + 1], *lower[join_dim + 2 :]
+    )
 
 
 def passed_along(value, axis, steps):
@@ -72,7 +89,22 @@
     stations = lax.axis_size("stn")
     halves = lax.axis_size("tm")
     scale = 1.0 / (spec_dev * halves)
-    moved = lax.all_to_all(spectra[None], ("stn", "tm"), split_axis=1, concat_axis=0, tiled=True)
+
+    def spot_state(block_here, mesh_ax, base_x, local_x):
+        taken_in = axis_size(mesh_ax)
+        odd = axis_index(mesh_ax)
+        wide_out, r1 = (taken_in, odd)
+        known = load_frames(block_here, base_x, wide_out)
+        column = [known[r1]]
+        for dev_i in range(1, wide_out):
+            r2 = known[r1 ^ dev_i]
+            d_next = ppermute(r2, mesh_ax, [(rr, rr ^ dev_i) for rr in range(wide_out)])
+            column.append(d_next)
+        opened = jnp.stack(column, axis=0)
+        known = opened[r1 ^ jnp.arange(wide_out)]
+        return detail_quotas_over_axis(known, local_x)
+
+    moved = spot_state(spectra[None], ("stn", "tm"), 1, 0)
     per_dev = moved.shape[1] // 2
     blocks = moved.reshape(stations, halves, per_dev, 2, inputs_dev, sub_count, spec_dev)
     result = correlate(arrange(blocks))

time: 516 us -> 396 us (0.77); the launches traced: 508 us -> 394 us
  blocking collectives: 134 us -> 0 us
  waiting for transfers between devices: 1.73 us -> 129 us
  local copies, waits for them, and re-layouts: 177 us -> 83.8 us
  other arithmetic: 159 us -> 123 us
  starting transfers between devices: 0.12 us -> 22.1 us
    all_to_all x1 -> x0, blocking collectives: 134 us -> none  [shards(): lax.all_to_all(spectra[None], ('stn', 'tm'), split_axis=1, concat_axis=0,...]
    ppermute x0 -> x15, waiting for transfers between devices: none -> 127 us  [spot_state(): d_next = ppermute(r2, mesh_ax, [(rr, rr ^ dev_i) for rr in range(wide_out)])]
    broadcast_in_dim x1 -> x0, local copies, waits for them, and re-layouts: 47.5 us -> none  [shards(): spectra[None]]
    all_to_all x1 -> x0, local copies, waits for them, and re-layouts: 36 us -> none  [shards(): lax.all_to_all(spectra[None], ('stn', 'tm'), split_axis=1, concat_axis=0,...]
    unnamed x1 -> x0, other arithmetic: 35.9 us -> none
    ppermute x0 -> x15, starting transfers between devices: none -> 22 us  [spot_state(): d_next = ppermute(r2, mesh_ax, [(rr, rr ^ dev_i) for rr in range(wide_out)])]
    another operation x0 -> x3, local copies, waits for them, and re-layouts: none -> 20.8 us  [the longest x2 20.1 us: shards(): moved.reshape(stations, halves, per_dev, 2, inputs_dev, sub_count, spec_dev)]
    unnamed x9 -> x20, local copies, waits for them, and re-layouts: 28 us -> 10.8 us
  transfers between devices with their start and end apart: 1 -> 16, of which waited for: 1 -> 11; matrix products, arithmetic and copies ran while one was open for 0% -> 3% of each run, Pallas kernels for 0% -> 0%
where the time goes in v1:
time: 396 us; the launch traced here: 394 us
  waiting for transfers between devices  129 us (33%)
  other arithmetic  123 us (31%)
  local copies, waits for them, and re-layouts  83.8 us (21%)
  matrix products  35.7 us (9%)
  starting transfers between devices  22.1 us (6%)
    ppermute x15, waiting for transfers between devices, spot_state(): d_next = ppermute(r2, mesh_ax, [(rr, rr ^ dev_i) for rr in range(wide_out)])  127 us
    add x1, other arithmetic, shards(): filtered + filter_taps[tap_index] * extended[:, :, tap_index:tap_index +...  74.6 us
    mul x1, other arithmetic, shards(): return result * scale  23.2 us
    ppermute x15, starting transfers between devices, spot_state(): d_next = ppermute(r2, mesh_ax, [(rr, rr ^ dev_i) for rr in range(wide_out)])  22 us
    another operation x2, local copies, waits for them, and re-layouts, shards(): moved.reshape(stations, halves, per_dev, 2, inputs_dev, sub_count, spec_dev)  20.1 us
    dot_general x1, matrix products, correlate(): jnp.einsum('gcis,gcjs->gcij', left_imag, right_side, preferred_element_ty...  14.1 us
    dot_general x1, matrix products, shards(): lax.dot_general(table, filtered.reshape(-1, frame_len), (((0,), (1,)), ((...  13.1 us
    unnamed x20, local copies, waits for them, and re-layouts  10.8 us
  transfers between devices with their start and end apart: 16, of which 11 were waited for; matrix products, arithmetic and copies ran while one was open for 3% of the time, Pallas kernels for 0%

profile of v1, /device:TPU:1, one launch (start us, length us, event | category | flops | bytes accessed | tf_op | source)
XLA Modules:
  0.0 393.8 jit_solution(11022148168677715255)
XLA Ops:
  0.0 9.0 %convert_element_type.26 = bf16[88,2,16384]{2,1,0:T(2,128)(2,1)} convert(s32[88,2,16384]{2,1,0:T(2,128)} %param.2) | non-fusion elementwise | flops 2883584 | bytes 17301504 | tf_op jit(solution)/shard_map/convert_element_type | solution.py:70
  9.0 10.5 %reshape.173 = bf16[88,2,128,128]{3,2,1,0:T(8,128)(2,1)} reshape(bf16[88,2,16384]{2,1,0:T(2,128)(2,1)} %convert_element_type.26) | data formatting | bytes 11534336 | tf_op jit(solution)/shard_map/reshape | solution.py:70
  21.8 1.6 collective-permute-done
  23.7 10.6 %maximum_convert_fusion = f32[88,2,143,128]{3,2,0,1:T(8,128)} fusion(bf16[88,2,15,128]{3,2,0,1:T(8,128)(2,1)S(1)} %pad_select_fusion, bf16[88,2,128,128]{3,2,1,0:T(8,128)(2,1)} %reshape.173), kind=kLoop, calls=%fused_computation.37 | loop fusion | flops 12886016 | bytes 19329024 | tf_op jit(solution)/shard_map/convert_element_type | solution.py:75
  34.3 74.6 %fusion.1 = f32[88,2,128,128]{3,2,0,1:T(8,128)} fusion(f32[88,2,143,128]{3,2,0,1:T(8,128)} %maximum_convert_fusion, f32[128]{0:T(128)S(1)} %get-tuple-element.39, f32[128]{0:T(128)S(1)} %get-tuple-element.40, f32[128]{0:T(128)S(1)} %get-tuple-element.26, f32[128]{0:T(128)S(1)} %get-tuple-element.27, f32[128]{0:T(128)S(1)} %get-tuple-element.28, ...), kind=kLoop, calls=%fused_computation.5 | loop fusion | flops 89391104 | bytes 196091904 | tf_op jit(solution)/shard_map/add | solution.py:79
  108.9 10.6 %copy.17 = f32[88,2,128,128]{3,2,1,0:T(8,128)} copy(f32[88,2,128,128]{3,2,0,1:T(8,128)} %fusion.1) | data formatting | bytes 23068672 | tf_op jit(solution)/shard_map/add | solution.py:79
  119.6 13.1 %fusion = bf16[16,1,8,22528]{3,2,0,1:T(8,128)(2,1)S(1)} fusion(f32[128,128]{0,1:T(8,128)S(1)} %bitcast.113, f32[22528,128]{1,0:T(8,128)} %bitcast.111), kind=kOutput, calls=%fused_computation.3 | convolution fusion | flops 4432068608 | bytes 17367040 | tf_op jit(solution)/shard_map/dot_general | solution.py:82
  134.4 5.7 %collective-permute-start.15 = (bf16[1,8,22528]{2,1,0:T(8,128)(2,1)S(1)}, bf16[1,8,22528]{2,1,0:T(8,128)(2,1)S(1)}, u32[]{:S(2)}, u32[]{:S(2)}) collective-permute-start(bf16[1,8,22528]{2,1,0:T(8,128)(2,1)S(1)} %get-tuple-element.7), channel_id=1, source_target_pairs={{0,15},{1,14},{2,13},{3,12},{4,11},{5,10},{6,9},{7,8},{8,7},{9,6},... | collective-permute-start | bytes 1081352 | tf_op jit(solution)/shard_map/ppermute | solution.py:101
  140.1 3.7 collective-permute-start.13
  145.8 18.7 %collective-permute-done.2 = bf16[1,8,22528]{2,1,0:T(8,128)(2,1)S(1)} collective-permute-done((bf16[1,8,22528]{2,1,0:T(8,128)(2,1)S(1)}, bf16[1,8,22528]{2,1,0:T(8,128)(2,1)S(1)}, u32[]{:S(2)}, u32[]{:S(2)}) %collective-permute-start.2) | collective-permute-done | bytes 360480 | tf_op jit(solution)/shard_map/ppermute | solution.py:101
  166.8 8.3 %collective-permute-done.3 = bf16[1,8,22528]{2,1,0:T(8,128)(2,1)S(1)} collective-permute-done((bf16[1,8,22528]{2,1,0:T(8,128)(2,1)S(1)}, bf16[1,8,22528]{2,1,0:T(8,128)(2,1)S(1)}, u32[]{:S(2)}, u32[]{:S(2)}) %collective-permute-start.3) | collective-permute-done | bytes 360480 | tf_op jit(solution)/shard_map/ppermute | solution.py:101
  175.9 8.8 %collective-permute-done.4 = bf16[1,8,22528]{2,1,0:T(8,128)(2,1)S(1)} collective-permute-done((bf16[1,8,22528]{2,1,0:T(8,128)(2,1)S(1)}, bf16[1,8,22528]{2,1,0:T(8,128)(2,1)S(1)}, u32[]{:S(2)}, u32[]{:S(2)}) %collective-permute-start.4) | collective-permute-done | bytes 360480 | tf_op jit(solution)/shard_map/ppermute | solution.py:101
  186.6 8.7 %collective-permute-done.5 = bf16[1,8,22528]{2,1,0:T(8,128)(2,1)S(1)} collective-permute-done((bf16[1,8,22528]{2,1,0:T(8,128)(2,1)S(1)}, bf16[1,8,22528]{2,1,0:T(8,128)(2,1)S(1)}, u32[]{:S(2)}, u32[]{:S(2)}) %collective-permute-start.5) | collective-permute-done | bytes 360480 | tf_op jit(solution)/shard_map/ppermute | solution.py:101
  195.2 1.9 collective-permute-start.6
  197.9 7.3 %collective-permute-done.6 = bf16[1,8,22528]{2,1,0:T(8,128)(2,1)S(1)} collective-permute-done((bf16[1,8,22528]{2,1,0:T(8,128)(2,1)S(1)}, bf16[1,8,22528]{2,1,0:T(8,128)(2,1)S(1)}, u32[]{:S(2)}, u32[]{:S(2)}) %collective-permute-start.6) | collective-permute-done | bytes 360480 | tf_op jit(solution)/shard_map/ppermute | solution.py:101
  205.2 3.6 collective-permute-start.7
  209.5 8.3 %collective-permute-done.7 = bf16[1,8,22528]{2,1,0:T(8,128)(2,1)S(1)} collective-permute-done((bf16[1,8,22528]{2,1,0:T(8,128)(2,1)S(1)}, bf16[1,8,22528]{2,1,0:T(8,128)(2,1)S(1)}, u32[]{:S(2)}, u32[]{:S(2)}) %collective-permute-start.7) | collective-permute-done | bytes 360480 | tf_op jit(solution)/shard_map/ppermute | solution.py:101
  217.9 3.0 collective-permute-start.8
  221.6 15.5 %collective-permute-done.8 = bf16[1,8,22528]{2,1,0:T(8,128)(2,1)S(1)} collective-permute-done((bf16[1,8,22528]{2,1,0:T(8,128)(2,1)S(1)}, bf16[1,8,22528]{2,1,0:T(8,128)(2,1)S(1)}, u32[]{:S(2)}, u32[]{:S(2)}) %collective-permute-start.8) | collective-permute-done | bytes 360480 | tf_op jit(solution)/shard_map/ppermute | solution.py:101
  237.9 18.6 %collective-permute-done.9 = bf16[1,8,22528]{2,1,0:T(8,128)(2,1)S(1)} collective-permute-done((bf16[1,8,22528]{2,1,0:T(8,128)(2,1)S(1)}, bf16[1,8,22528]{2,1,0:T(8,128)(2,1)S(1)}, u32[]{:S(2)}, u32[]{:S(2)}) %collective-permute-start.9) | collective-permute-done | bytes 360480 | tf_op jit(solution)/shard_map/ppermute | solution.py:101
  257.3 16.6 %collective-permute-done.10 = bf16[1,8,22528]{2,1,0:T(8,128)(2,1)S(1)} collective-permute-done((bf16[1,8,22528]{2,1,0:T(8,128)(2,1)S(1)}, bf16[1,8,22528]{2,1,0:T(8,128)(2,1)S(1)}, u32[]{:S(2)}, u32[]{:S(2)}) %collective-permute-start.10) | collective-permute-done | bytes 360480 | tf_op jit(solution)/shard_map/ppermute | solution.py:101
  274.7 16.6 %collective-permute-done.11 = bf16[1,8,22528]{2,1,0:T(8,128)(2,1)S(1)} collective-permute-done((bf16[1,8,22528]{2,1,0:T(8,128)(2,1)S(1)}, bf16[1,8,22528]{2,1,0:T(8,128)(2,1)S(1)}, u32[]{:S(2)}, u32[]{:S(2)}) %collective-permute-start.11) | collective-permute-done | bytes 360480 | tf_op jit(solution)/shard_map/ppermute | solution.py:101
  295.1 6.0 %gather_fusion = bf16[16,8,22528]{2,1,0:T(8,128)(2,1)} fusion(bf16[16,8,22528]{2,1,0:T(8,128)(2,1)} %bitcast.49, s32[1024]{0:T(1024)S(1)} %pad_clamp_fusion), kind=kCustom, calls=%fused_computation | custom fusion | bytes 11534400 | tf_op jit(solution)/shard_map/gather | solution.py:104
  301.2 8.9 %reshape_reshape.3 = bf16[8,2,4,2,88,2,128]{6,5,4,3,2,1,0:T(2,128)(2,1)} reshape(bf16[16,8,22528]{2,1,0:T(8,128)(2,1)} %gather_fusion) | data formatting | bytes 11534336 | tf_op jit(solution)/shard_map/reshape;reshape | solution.py:109
  310.1 11.2 %copy.25 = bf16[8,2,4,2,88,2,128]{6,1,4,0,2,5,3:T(2,128)(2,1)S(1)} copy(bf16[8,2,4,2,88,2,128]{6,5,4,3,2,1,0:T(2,128)(2,1)} %reshape_reshape.3) | data formatting | bytes 11534336 | tf_op jit(solution)/shard_map/reshape;reshape | solution.py:109
  321.3 7.7 %fusion.27 = (bf16[1,2,4,8,88,2,128]{6,5,4,3,2,1,0:T(2,128)(2,1)}, bf16[1,2,4,8,88,2,128]{6,5,4,3,2,1,0:T(2,128)(2,1)}) fusion(bf16[2,2,4,8,88,2,128]{6,5,4,3,2,1,0:T(2,128)(2,1)S(1)} %bitcast.112), kind=kLoop, calls=%fused_computation.109 | loop fusion | bytes 11534336 | tf_op jit(solution)/shard_map/slice | solution.py:52
  329.0 6.4 %squeeze.67 = bf16[2,4,704,256]{3,2,1,0:T(8,128)(2,1)S(1)} reshape(bf16[1,2,4,8,88,2,128]{6,5,4,3,2,1,0:T(2,128)(2,1)} %get-tuple-element.5) | data formatting | bytes 5767168 | tf_op jit(solution)/shard_map/squeeze | solution.py:52
  335.3 7.4 %squeeze.66 = bf16[2,4,704,256]{3,2,1,0:T(8,128)(2,1)} reshape(bf16[1,2,4,8,88,2,128]{6,5,4,3,2,1,0:T(2,128)(2,1)} %get-tuple-element.6) | data formatting | bytes 5767168 | tf_op jit(solution)/shard_map/squeeze | solution.py:51
  342.8 5.0 %fusion.28 = (bf16[2,4,704,256]{3,2,1,0:T(8,128)(2,1)}, bf16[2,4,704,512]{3,2,1,0:T(8,128)(2,1)S(1)}) fusion(bf16[2,4,704,256]{3,2,1,0:T(8,128)(2,1)} %squeeze.66), kind=kLoop, calls=%fused_computation.110 | loop fusion | flops 4325375 | bytes 8650752 | tf_op jit(solution)/shard_map/neg | solution.py:54
  348.1 8.4 %convolution_bitcast_fusion.1 = f32[1,2,4,704,704]{4,3,2,1,0:T(8,128)} fusion(bf16[2,4,704,512]{3,2,1,0:T(8,128)(2,1)S(1)} %constant_dynamic-update-slice_fusion), kind=kOutput, calls=%fused_computation.36 | convolution fusion | flops 4060086272 | bytes 21626880 | tf_op jit(solution)/shard_map/gcis,gcjs->gcij/dot_general | solution.py:55
  356.5 14.1 %convolution_bitcast_fusion = f32[1,2,4,704,704]{4,3,2,1,0:T(8,128)} fusion(bf16[2,4,704,512]{3,2,1,0:T(8,128)(2,1)} %copy-done, bf16[2,4,704,256]{3,2,1,0:T(8,128)(2,1)} %get-tuple-element.23, bf16[2,4,704,256]{3,2,1,0:T(8,128)(2,1)S(1)} %squeeze.67), kind=kOutput, calls=%fused_computation.35 | convolution fusion | flops 4071620608 | bytes 27394048 | tf_op jit(solution)/shard_map/gcis,gcjs->gcij/dot_general | solution.py:58
  370.6 23.2 %maximum_multiply_fusion = f32[2,2,4,704,704]{4,3,2,1,0:T(8,128)} fusion(f32[1,2,4,704,704]{4,3,2,1,0:T(8,128)} %convolution_bitcast_fusion, f32[1,2,4,704,704]{4,3,2,1,0:T(8,128)} %convolution_bitcast_fusion.1), kind=kLoop, calls=%fused_computation.1 | loop fusion | flops 15859712 | bytes 63438848 | tf_op jit(solution)/shard_map/mul | solution.py:111
  (50 shorter events, 19.6 us)
Async XLA Ops:
  9.0 12.8 %copy-start.1 = (f32[16,128]{1,0:T(8,128)S(1)}, f32[16,128]{1,0:T(8,128)}, u32[]{:S(2)}) copy-start(f32[16,128]{1,0:T(8,128)} %param.3) | copy-start | bytes 24580
  21.2 2.2 collective-permute-start
  134.2 9.6 %collective-permute-start.1 = (bf16[1,8,22528]{2,1,0:T(8,128)(2,1)S(1)}, bf16[1,8,22528]{2,1,0:T(8,128)(2,1)S(1)}, u32[]{:S(2)}, u32[]{:S(2)}) collective-permute-start(bf16[1,8,22528]{2,1,0:T(8,128)(2,1)S(1)} %get-tuple-element.21), channel_id=1, source_target_pairs={{0,1},{1,0},{2,3},{3,2},{4,5},{5,4},{6,7},{7,6},{8,9},{9,8},{10,11... | collective-permute-start | bytes 1081352 | tf_op jit(solution)/shard_map/ppermute | solution.py:101
  134.4 160.0 %collective-permute-start.15 = (bf16[1,8,22528]{2,1,0:T(8,128)(2,1)S(1)}, bf16[1,8,22528]{2,1,0:T(8,128)(2,1)S(1)}, u32[]{:S(2)}, u32[]{:S(2)}) collective-permute-start(bf16[1,8,22528]{2,1,0:T(8,128)(2,1)S(1)} %get-tuple-element.7), channel_id=1, source_target_pairs={{0,15},{1,14},{2,13},{3,12},{4,11},{5,10},{6,9},{7,8},{8,7},{9,6},... | collective-permute-start | bytes 1081352 | tf_op jit(solution)/shard_map/ppermute | solution.py:101
  140.1 153.5 %collective-permute-start.14 = (bf16[1,8,22528]{2,1,0:T(8,128)(2,1)S(1)}, bf16[1,8,22528]{2,1,0:T(8,128)(2,1)S(1)}, u32[]{:S(2)}, u32[]{:S(2)}) collective-permute-start(bf16[1,8,22528]{2,1,0:T(8,128)(2,1)S(1)} %get-tuple-element.8), channel_id=1, source_target_pairs={{0,14},{1,15},{2,12},{3,13},{4,10},{5,11},{6,8},{7,9},{8,6},{9,7},... | collective-permute-start | bytes 1081352 | tf_op jit(solution)/shard_map/ppermute | solution.py:101
  140.1 152.7 %collective-permute-start.13 = (bf16[1,8,22528]{2,1,0:T(8,128)(2,1)S(1)}, bf16[1,8,22528]{2,1,0:T(8,128)(2,1)S(1)}, u32[]{:S(2)}, u32[]{:S(2)}) collective-permute-start(bf16[1,8,22528]{2,1,0:T(8,128)(2,1)S(1)} %get-tuple-element.9), channel_id=1, source_target_pairs={{0,13},{1,12},{2,15},{3,14},{4,9},{5,8},{6,11},{7,10},{8,5},{9,4},... | collective-permute-start | bytes 1081352 | tf_op jit(solution)/shard_map/ppermute | solution.py:101
  143.8 148.2 %collective-permute-start.12 = (bf16[1,8,22528]{2,1,0:T(8,128)(2,1)S(1)}, bf16[1,8,22528]{2,1,0:T(8,128)(2,1)S(1)}, u32[]{:S(2)}, u32[]{:S(2)}) collective-permute-start(bf16[1,8,22528]{2,1,0:T(8,128)(2,1)S(1)} %get-tuple-element.10), channel_id=1, source_target_pairs={{0,12},{1,13},{2,14},{3,15},{4,8},{5,9},{6,10},{7,11},{8,4},{9,5},... | collective-permute-start | bytes 1081352 | tf_op jit(solution)/shard_map/ppermute | solution.py:101
  143.8 20.7 %collective-permute-start.2 = (bf16[1,8,22528]{2,1,0:T(8,128)(2,1)S(1)}, bf16[1,8,22528]{2,1,0:T(8,128)(2,1)S(1)}, u32[]{:S(2)}, u32[]{:S(2)}) collective-permute-start(bf16[1,8,22528]{2,1,0:T(8,128)(2,1)S(1)} %get-tuple-element.20), channel_id=1, source_target_pairs={{0,2},{1,3},{2,0},{3,1},{4,6},{5,7},{6,4},{7,5},{8,10},{9,11},{10,... | collective-permute-start | bytes 1081352 | tf_op jit(solution)/shard_map/ppermute | solution.py:101
  164.5 10.6 %collective-permute-start.3 = (bf16[1,8,22528]{2,1,0:T(8,128)(2,1)S(1)}, bf16[1,8,22528]{2,1,0:T(8,128)(2,1)S(1)}, u32[]{:S(2)}, u32[]{:S(2)}) collective-permute-start(bf16[1,8,22528]{2,1,0:T(8,128)(2,1)S(1)} %get-tuple-element.19), channel_id=1, source_target_pairs={{0,3},{1,2},{2,1},{3,0},{4,7},{5,6},{6,5},{7,4},{8,11},{9,10},{10,... | collective-permute-start | bytes 1081352 | tf_op jit(solution)/shard_map/ppermute | solution.py:101
  175.1 9.6 %collective-permute-start.4 = (bf16[1,8,22528]{2,1,0:T(8,128)(2,1)S(1)}, bf16[1,8,22528]{2,1,0:T(8,128)(2,1)S(1)}, u32[]{:S(2)}, u32[]{:S(2)}) collective-permute-start(bf16[1,8,22528]{2,1,0:T(8,128)(2,1)S(1)} %get-tuple-element.18), channel_id=1, source_target_pairs={{0,4},{1,5},{2,6},{3,7},{4,0},{5,1},{6,2},{7,3},{8,12},{9,13},{10,... | collective-permute-start | bytes 1081352 | tf_op jit(solution)/shard_map/ppermute | solution.py:101
  184.7 10.5 %collective-permute-start.5 = (bf16[1,8,22528]{2,1,0:T(8,128)(2,1)S(1)}, bf16[1,8,22528]{2,1,0:T(8,128)(2,1)S(1)}, u32[]{:S(2)}, u32[]{:S(2)}) collective-permute-start(bf16[1,8,22528]{2,1,0:T(8,128)(2,1)S(1)} %get-tuple-element.17), channel_id=1, source_target_pairs={{0,5},{1,4},{2,7},{3,6},{4,1},{5,0},{6,3},{7,2},{8,13},{9,12},{10,... | collective-permute-start | bytes 1081352 | tf_op jit(solution)/shard_map/ppermute | solution.py:101
  195.2 10.0 %collective-permute-start.6 = (bf16[1,8,22528]{2,1,0:T(8,128)(2,1)S(1)}, bf16[1,8,22528]{2,1,0:T(8,128)(2,1)S(1)}, u32[]{:S(2)}, u32[]{:S(2)}) collective-permute-start(bf16[1,8,22528]{2,1,0:T(8,128)(2,1)S(1)} %get-tuple-element.16), channel_id=1, source_target_pairs={{0,6},{1,7},{2,4},{3,5},{4,2},{5,3},{6,0},{7,1},{8,14},{9,15},{10,... | collective-permute-start | bytes 1081352 | tf_op jit(solution)/shard_map/ppermute | solution.py:101
  205.2 12.7 %collective-permute-start.7 = (bf16[1,8,22528]{2,1,0:T(8,128)(2,1)S(1)}, bf16[1,8,22528]{2,1,0:T(8,128)(2,1)S(1)}, u32[]{:S(2)}, u32[]{:S(2)}) collective-permute-start(bf16[1,8,22528]{2,1,0:T(8,128)(2,1)S(1)} %get-tuple-element.15), channel_id=1, source_target_pairs={{0,7},{1,6},{2,5},{3,4},{4,3},{5,2},{6,1},{7,0},{8,15},{9,14},{10,... | collective-permute-start | bytes 1081352 | tf_op jit(solution)/shard_map/ppermute | solution.py:101
  217.9 19.3 %collective-permute-start.8 = (bf16[1,8,22528]{2,1,0:T(8,128)(2,1)S(1)}, bf16[1,8,22528]{2,1,0:T(8,128)(2,1)S(1)}, u32[]{:S(2)}, u32[]{:S(2)}) collective-permute-start(bf16[1,8,22528]{2,1,0:T(8,128)(2,1)S(1)} %get-tuple-element.14), channel_id=1, source_target_pairs={{0,8},{1,9},{2,10},{3,11},{4,12},{5,13},{6,14},{7,15},{8,0},{9,1},... | collective-permute-start | bytes 1081352 | tf_op jit(solution)/shard_map/ppermute | solution.py:101
  237.2 19.3 %collective-permute-start.9 = (bf16[1,8,22528]{2,1,0:T(8,128)(2,1)S(1)}, bf16[1,8,22528]{2,1,0:T(8,128)(2,1)S(1)}, u32[]{:S(2)}, u32[]{:S(2)}) collective-permute-start(bf16[1,8,22528]{2,1,0:T(8,128)(2,1)S(1)} %get-tuple-element.13), channel_id=1, source_target_pairs={{0,9},{1,8},{2,11},{3,10},{4,13},{5,12},{6,15},{7,14},{8,1},{9,0},... | collective-permute-start | bytes 1081352 | tf_op jit(solution)/shard_map/ppermute | solution.py:101
  256.5 17.4 %collective-permute-start.10 = (bf16[1,8,22528]{2,1,0:T(8,128)(2,1)S(1)}, bf16[1,8,22528]{2,1,0:T(8,128)(2,1)S(1)}, u32[]{:S(2)}, u32[]{:S(2)}) collective-permute-start(bf16[1,8,22528]{2,1,0:T(8,128)(2,1)S(1)} %get-tuple-element.12), channel_id=1, source_target_pairs={{0,10},{1,11},{2,8},{3,9},{4,14},{5,15},{6,12},{7,13},{8,2},{9,3},... | collective-permute-start | bytes 1081352 | tf_op jit(solution)/shard_map/ppermute | solution.py:101
  273.9 17.4 %collective-permute-start.11 = (bf16[1,8,22528]{2,1,0:T(8,128)(2,1)S(1)}, bf16[1,8,22528]{2,1,0:T(8,128)(2,1)S(1)}, u32[]{:S(2)}, u32[]{:S(2)}) collective-permute-start(bf16[1,8,22528]{2,1,0:T(8,128)(2,1)S(1)} %get-tuple-element.11), channel_id=1, source_target_pairs={{0,11},{1,10},{2,9},{3,8},{4,15},{5,14},{6,13},{7,12},{8,3},{9,2},... | collective-permute-start | bytes 1081352 | tf_op jit(solution)/shard_map/ppermute | solution.py:101
  348.1 8.4 %copy-start = (bf16[2,4,704,512]{3,2,1,0:T(8,128)(2,1)}, bf16[2,4,704,512]{3,2,1,0:T(8,128)(2,1)S(1)}, u32[]{:S(2)}) copy-start(bf16[2,4,704,512]{3,2,1,0:T(8,128)(2,1)S(1)} %constant_dynamic-update-slice_fusion) | copy-start | bytes 17301508
